TPU v7x, 32 devices: a whole 2x2x4 slice. The times are simulated.
32 devices in a mesh: dp: 2 (over x), expert: 16 (over z, y, core).
Axes of the slice: x: 2, y: 2, z: 4, core: 2. Of those that a mesh axis runs over, the one named last changes fastest.
Arguments:
- tokens: bfloat16 [2, 512, 4096], P(None, ('dp', 'expert')), may hold values from -6 to 6
- expert_ids: int32 [2, 512, 8], P(None, ('dp', 'expert')), may hold values from 0 to 15, all different within a row; in each aligned block of 16 rows (0 to 15, 16 to 31, ..., all dimensions but the last counted through in order) at most 9 rows name the same one
- gate_probs: float32 [2, 512, 8], P(None, ('dp', 'expert')), may hold values from 0.1 to 1
- gate_up: bfloat16 [16, 2, 768, 4096], P('expert', None, 'dp'), may hold values from -0.09375 to 0.09375
- down_proj: bfloat16 [16, 768, 4096], P('expert', 'dp'), may hold values from -0.21875 to 0.21875
- pairs: int32 [2, 2], replicated, may hold values from 0 to 15, as said below
Outputs:
- moe_out: bfloat16 [2, 512, 4096], P(None, ('dp', 'expert'))
- placed_gate_up: bfloat16 [16, 2, 768, 4096], P('expert', None, 'dp')
- placed_down: bfloat16 [16, 768, 4096], P('expert', 'dp')
Inputs may be any that keep to these rules, and one draw needn't show every extreme that they name: `expert_ids`: in each step, the 16 rows of one device name one expert at most 9 times. `pairs`: each row is (j, j + 8) with j below 8; no slot stands in two rows.
All inputs are finite; a program needn't handle non-finite values.
Results may differ from a plain program's by a relative error of at most 0.012.
Values may be sent and summed in bfloat16 or wider, within the bound.
A program may use at most 128 MiB of HBM per device.

v0:
```python
import jax
import jax.numpy as jnp
from jax import lax
from jax.sharding import PartitionSpec as P


def from_partner(shard, axis, distance):
    return lax.ppermute(shard, axis, [(i, i ^ 1 << distance) for i in range(lax.axis_size(axis))])


def route_slots(step_ids, place_map, capacity):
    n_slots_dev = place_map.shape[0]
    positions = lax.iota(jnp.int32, n_slots_dev)
    dest_pos = jnp.sum(jnp.where(step_ids[..., None] == positions, place_map, 0), axis=-1)
    flat_dest = dest_pos.reshape(-1)
    onehot = (flat_dest[:, None] == positions).astype(jnp.int32)
    before = jnp.cumsum(onehot, axis=0) - onehot
    slot_rank = jnp.sum(before * onehot, axis=1)
    return flat_dest * capacity + slot_rank


def pack_rows(step_tokens, slot_ids, slot_count, top_count):
    slot_hot = (slot_ids[:, None] == lax.iota(jnp.int32, slot_count)).astype(jnp.bfloat16)
    slot_hot = slot_hot.reshape(step_tokens.shape[0], top_count, slot_count).sum(axis=1)
    return jnp.einsum(
        "rk,rd->kd", slot_hot, step_tokens, preferred_element_type=jnp.float32
    ).astype(jnp.bfloat16)


def expert_partial(row_block, expert_gu, expert_down):
    unit_count = expert_down.shape[0]
    stacked = expert_gu.reshape(2 * unit_count, expert_gu.shape[2])
    projected = lax.dot_general(
        row_block, stacked, (((1,), (1,)), ((), ())), preferred_element_type=jnp.float32
    )
    hidden = (jax.nn.silu(projected[:, :unit_count]) * projected[:, unit_count:]).astype(
        jnp.bfloat16
    )
    return jnp.dot(hidden, expert_down, preferred_element_type=jnp.float32).astype(jnp.bfloat16)


def run_steps(step_tokens, step_ids, step_gates, places, stack_gu, stack_down, capacity):
    step_count, row_count, feature_dim = step_tokens.shape
    top_count = step_ids.shape[2]
    slot_dev = places.shape[1]
    slot_count = slot_dev * capacity
    own_slots = route_slots(step_ids[0], places[0], capacity)
    packed = jnp.stack([pack_rows(step_tokens[0], own_slots, slot_count, top_count)])
    packed = packed.reshape(step_count, slot_dev, capacity, feature_dim)
    arrived = lax.all_to_all(packed, "expert", split_axis=1, concat_axis=1, tiled=True)
    received = lax.all_gather(arrived[:, None], "dp", axis=1, tiled=True)
    groups = received.shape[1]
    partial_value = jnp.stack(
        [expert_partial(received[0].reshape(-1, feature_dim), stack_gu[0], stack_down[0])]
    )
    partial_value = partial_value.reshape(step_count, groups, slot_dev, capacity, feature_dim)
    summed = lax.psum_scatter(partial_value, "dp", scatter_dimension=1, tiled=True).astype(
        jnp.float32
    )
    expert_out = summed.astype(jnp.bfloat16).reshape(step_count, slot_dev, capacity, feature_dim)
    returned = lax.all_to_all(
        expert_out, "expert", split_axis=1, concat_axis=1, tiled=True
    ).reshape(step_count, slot_count, feature_dim)
    picked = jnp.take(returned[0], own_slots, axis=0).astype(jnp.float32)
    picked = picked.reshape(row_count, top_count, feature_dim)
    mixed = jnp.sum(step_gates[0][..., None] * picked, axis=1)
    results = [mixed.astype(jnp.bfloat16)]
    return jnp.stack(results)


def local(tokens, expert_ids, gate_probs, gate_up, down_proj, pairs):
    slot_dev = lax.axis_size("expert")
    device_pos = lax.axis_index("expert")
    row_count = tokens.shape[1]
    top_count = expert_ids.shape[2]
    capacity = min(row_count, max(2, row_count * top_count // slot_dev + 1))
    positions = lax.iota(jnp.int32, slot_dev)
    lower_dev = pairs[:, 0]
    upper_dev = pairs[:, 1]
    shifted = positions + jnp.sum(
        jnp.where(positions[:, None] == lower_dev[None, :], (upper_dev - lower_dev)[None, :], 0),
        axis=1,
    )
    shifted = shifted + jnp.sum(
        jnp.where(positions[:, None] == upper_dev[None, :], (lower_dev - upper_dev)[None, :], 0),
        axis=1,
    )
    moving = jnp.any(pairs == device_pos)
    partner_bit = slot_dev.bit_length() - 2
    step_one = run_steps(
        tokens[:1], expert_ids[:1], gate_probs[:1], positions[None], gate_up, down_proj, capacity
    )
    got_gu, got_down = from_partner((gate_up, down_proj), "expert", partner_bit)
    new_gu = jnp.where(moving, got_gu, gate_up)
    new_down = jnp.where(moving, got_down, down_proj)
    step_two = run_steps(
        tokens[1:], expert_ids[1:], gate_probs[1:], shifted[None], new_gu, new_down, capacity
    )
    results = jnp.concatenate([step_one, step_two])
    return (results, new_gu, new_down)


def solution(mesh):
    return jax.shard_map(
        local,
        mesh=mesh,
        in_specs=(
            P(None, ("dp", "expert"), None),
            P(None, ("dp", "expert"), None),
            P(None, ("dp", "expert"), None),
            P("expert", None, "dp", None),
            P("expert", "dp", None),
            P(),
        ),
        out_specs=(
            P(None, ("dp", "expert"), None),
            P("expert", None, "dp", None),
            P("expert", "dp", None),
        ),
        check_vma=False,
    )
```

profile of v0, /device:TPU:0, one launch (start us, length us, event | category | flops | bytes accessed | tf_op | source)
XLA Modules:
  0.0 671.8 jit_solution(7235432803878191632)
XLA Ops:
  9.1 1.4 convolution_convert_fusion.3
  10.5 1.6 reshape_stack.12
  12.1 7.5 %all-to-all-start = ((bf16[1,16,9,4096]{3,2,0,1:T(8,128)(2,1)}), bf16[1,16,9,4096]{3,2,0,1:T(8,128)(2,1)S(1)}, u32[]{:S(2)}, u32[]{:S(2)}) async-start(bf16[1,16,9,4096]{3,2,0,1:T(8,128)(2,1)} %bitcast.52), calls=%async_computation | async-start | bytes 4194304 | tf_op jit(solution)/shard_map/all_to_all | solution.py:50
  21.3 39.5 %all-to-all-done = bf16[1,16,9,4096]{3,2,0,1:T(8,128)(2,1)S(1)} async-done(((bf16[1,16,9,4096]{3,2,0,1:T(8,128)(2,1)}), bf16[1,16,9,4096]{3,2,0,1:T(8,128)(2,1)S(1)}, u32[]{:S(2)}, u32[]{:S(2)}) %all-to-all-start) | async-done | bytes 1179680 | tf_op jit(solution)/shard_map/all_to_all | solution.py:50
  60.8 1.7 copy.32
  63.0 1.6 reshape_stack.14
  64.6 11.2 %all-to-all-start.2 = ((bf16[1,16,9,4096]{3,2,0,1:T(8,128)(2,1)}), bf16[1,16,9,4096]{3,2,0,1:T(8,128)(2,1)S(1)}, u32[]{:S(2)}, u32[]{:S(2)}) async-start(bf16[1,16,9,4096]{3,2,0,1:T(8,128)(2,1)} %bitcast.53), calls=%async_computation.3 | async-start | bytes 4194304 | tf_op jit(solution)/shard_map/all_to_all | solution.py:50
  75.9 2.9 collective-permute-start
  78.8 173.0 %all-to-all-done.2 = bf16[1,16,9,4096]{3,2,0,1:T(8,128)(2,1)S(1)} async-done(((bf16[1,16,9,4096]{3,2,0,1:T(8,128)(2,1)}), bf16[1,16,9,4096]{3,2,0,1:T(8,128)(2,1)S(1)}, u32[]{:S(2)}, u32[]{:S(2)}) %all-to-all-start.2) | async-done | bytes 1179680 | tf_op jit(solution)/shard_map/all_to_all | solution.py:50
  251.7 1.8 copy.38
  253.6 9.9 %collective-permute-start.1 = (bf16[1,384,4096]{2,1,0:T(8,128)(2,1)}, bf16[1,384,4096]{2,1,0:T(8,128)(2,1)}, u32[]{:S(2)}, u32[]{:S(2)}) collective-permute-start(bf16[1,384,4096]{2,1,0:T(8,128)(2,1)} %param.12), channel_id=1, source_target_pairs={{0,8},{1,9},{2,10},{3,11},{4,12},{5,13},{6,14},{7,15},{8,0},{9,1},... | collective-permute-start | bytes 9437192 | tf_op jit(solution)/shard_map/ppermute | solution.py:8
  263.5 5.2 copy.33
  268.7 4.7 reshape_squeeze.12
  273.4 5.7 fusion.25
  279.1 2.8 convolution_convert_fusion.1
  281.9 4.6 reshape_stack.13
  287.4 242.0 %collective-permute-done.1 = bf16[1,384,4096]{2,1,0:T(8,128)(2,1)} collective-permute-done((bf16[1,384,4096]{2,1,0:T(8,128)(2,1)}, bf16[1,384,4096]{2,1,0:T(8,128)(2,1)}, u32[]{:S(2)}, u32[]{:S(2)}) %collective-permute-start.1) | collective-permute-done | bytes 3145760 | tf_op jit(solution)/shard_map/ppermute | solution.py:8
  529.5 4.5 broadcast_select_fusion.1
  534.0 5.2 copy.39
  539.2 4.7 reshape_squeeze.14
  543.9 4.1 broadcast_select_fusion
  548.0 5.6 fusion.26
  553.7 2.8 convolution_convert_fusion
  556.5 4.6 reshape_stack.15
  561.2 3.7 all-to-all-start.1
  564.9 49.0 %reduce-scatter.5.cloned.1.call-done = bf16[1,1,16,9,4096]{4,3,2,1,0:T(8,128)(2,1)} async-done(((bf16[1,2,16,9,4096]{4,3,2,1,0:T(8,128)(2,1)}), bf16[1,1,16,9,4096]{4,3,2,1,0:T(8,128)(2,1)}) %reduce-scatter.5.cloned.1.call-update) | async-done | bytes 1179664 | tf_op jit(solution)/shard_map/reduce_scatter | solution.py:57
  613.9 1.4 copy-done
  615.2 5.6 all-to-all-start.3
  621.1 1.8 squeeze_reshape.6
  622.9 2.2 gather_fusion
  625.1 2.1 fusion.3
  627.1 34.8 %all-to-all-done.3 = bf16[1,16,9,4096]{3,2,0,1:T(8,128)(2,1)S(1)} async-done(((bf16[1,16,9,4096]{3,2,0,1:T(8,128)(2,1)}), bf16[1,16,9,4096]{3,2,0,1:T(8,128)(2,1)S(1)}, u32[]{:S(2)}, u32[]{:S(2)}) %all-to-all-start.3) | async-done | bytes 1179680 | tf_op jit(solution)/shard_map/all_to_all | solution.py:61
  (62 shorter events, 8.5 us)
Async XLA Ops:
  12.1 7.7 %copy-start.5 = (s32[2,2]{1,0:T(2,128)S(1)}, s32[2,2]{1,0:T(2,128)}, u32[]{:S(2)}) copy-start(s32[2,2]{1,0:T(2,128)} %param.13) | copy-start | bytes 52
  12.1 48.6 %all-to-all-start = ((bf16[1,16,9,4096]{3,2,0,1:T(8,128)(2,1)}), bf16[1,16,9,4096]{3,2,0,1:T(8,128)(2,1)S(1)}, u32[]{:S(2)}, u32[]{:S(2)}) async-start(bf16[1,16,9,4096]{3,2,0,1:T(8,128)(2,1)} %bitcast.52), calls=%async_computation | async-start | bytes 4194304 | tf_op jit(solution)/shard_map/all_to_all | solution.py:50
  19.6 243.8 %all-gather.5.cloned.1.call-start = ((), (), s32[]{:S(2)}) async-start(), calls=%async_computation.8 | async-start | bytes 3538944 | tf_op jit(solution)/shard_map/all_gather | solution.py:51
  20.7 41.8 %copy-start.4 = (bf16[2,16,4096]{2,1,0:T(8,128)(2,1)S(1)}, bf16[2,16,4096]{2,1,0:T(8,128)(2,1)}, u32[]{:S(2)}) copy-start(bf16[2,16,4096]{2,1,0:T(8,128)(2,1)} %param.8) | copy-start | bytes 786436
  64.6 187.2 %all-to-all-start.2 = ((bf16[1,16,9,4096]{3,2,0,1:T(8,128)(2,1)}), bf16[1,16,9,4096]{3,2,0,1:T(8,128)(2,1)S(1)}, u32[]{:S(2)}, u32[]{:S(2)}) async-start(bf16[1,16,9,4096]{3,2,0,1:T(8,128)(2,1)} %bitcast.53), calls=%async_computation.3 | async-start | bytes 4194304 | tf_op jit(solution)/shard_map/all_to_all | solution.py:50
  75.8 458.2 %all-gather.7.cloned.1.call-start = ((), (), s32[]{:S(2)}) async-start(), calls=%async_computation.9 | async-start | bytes 3538944 | tf_op jit(solution)/shard_map/all_gather | solution.py:51
  75.9 468.0 %collective-permute-start = (bf16[1,2,384,4096]{3,2,1,0:T(8,128)(2,1)}, bf16[1,2,384,4096]{3,2,1,0:T(8,128)(2,1)}, u32[]{:S(2)}, u32[]{:S(2)}) collective-permute-start(bf16[1,2,384,4096]{3,2,1,0:T(8,128)(2,1)} %param.11), channel_id=1, source_target_pairs={{0,8},{1,9},{2,10},{3,11},{4,12},{5,13},{6,14},{7,15},{8,0},{9,1},... | collective-permute-start | bytes 18874376 | tf_op jit(solution)/shard_map/ppermute | solution.py:8
  253.5 307.6 %reduce-scatter.3.cloned.1.call-start = ((), (), s32[]{:S(2)}) async-start(), calls=%async_computation.6 | async-start | bytes 6291456 | tf_op jit(solution)/shard_map/reduce_scatter | solution.py:57
  253.6 275.9 %collective-permute-start.1 = (bf16[1,384,4096]{2,1,0:T(8,128)(2,1)}, bf16[1,384,4096]{2,1,0:T(8,128)(2,1)}, u32[]{:S(2)}, u32[]{:S(2)}) collective-permute-start(bf16[1,384,4096]{2,1,0:T(8,128)(2,1)} %param.12), channel_id=1, source_target_pairs={{0,8},{1,9},{2,10},{3,11},{4,12},{5,13},{6,14},{7,15},{8,0},{9,1},... | collective-permute-start | bytes 9437192 | tf_op jit(solution)/shard_map/ppermute | solution.py:8
  273.4 5.7 copy-start.2
  286.6 327.3 %reduce-scatter.5.cloned.1.call-start = ((), (), s32[]{:S(2)}) async-start(), calls=%async_computation.7 | async-start | bytes 6291456 | tf_op jit(solution)/shard_map/reduce_scatter | solution.py:57
  548.0 5.7 copy-start.1
  548.0 5.7 copy-start.3
  561.2 52.7 %all-to-all-start.1 = ((bf16[1,16,9,4096]{3,2,0,1:T(8,128)(2,1)}), bf16[1,16,9,4096]{3,2,0,1:T(8,128)(2,1)S(1)}, u32[]{:S(2)}, u32[]{:S(2)}) async-start(bf16[1,16,9,4096]{3,2,0,1:T(8,128)(2,1)} %bitcast.56), calls=%async_computation.2 | async-start | bytes 4194304 | tf_op jit(solution)/shard_map/all_to_all | solution.py:61
  564.9 55.9 %copy-start.6 = (f32[2,16,8]{1,2,0:T(8,128)S(1)}, f32[2,16,8]{1,2,0:T(8,128)}, u32[]{:S(2)}) copy-start(f32[2,16,8]{1,2,0:T(8,128)} %param.10) | copy-start | bytes 3076
  613.9 1.4 copy-start
  615.2 46.7 %all-to-all-start.3 = ((bf16[1,16,9,4096]{3,2,0,1:T(8,128)(2,1)}), bf16[1,16,9,4096]{3,2,0,1:T(8,128)(2,1)S(1)}, u32[]{:S(2)}, u32[]{:S(2)}) async-start(bf16[1,16,9,4096]{3,2,0,1:T(8,128)(2,1)} %bitcast.57), calls=%async_computation.5 | async-start | bytes 4194304 | tf_op jit(solution)/shard_map/all_to_all | solution.py:61
Sparse Core Ops, SparseCore 0:
  62.6 42.5 all-gather.4
  253.6 42.9 all-gather.6
  299.0 54.2 reduce-scatter.2
  561.3 52.5 reduce-scatter.4
where the time goes:
time: 678 us; the launch traced here: 672 us
  waiting for transfers between devices  538 us (79%)
  local copies, waits for them, and re-layouts  44.3 us (7%)
  starting transfers between devices  41.2 us (6%)
  matrix products  18.8 us (3%)
  other arithmetic  15 us (2%)
  between operations  14 us (2%)
    ppermute x2, waiting for transfers between devices, from_partner(): lax.ppermute(shard, axis, [(i, i ^ 1 << distance) for i in range(lax.axis...  242 us
    all_to_all x2, waiting for transfers between devices, run_steps(): lax.all_to_all(packed, 'expert', split_axis=1, concat_axis=1, tiled=True)  212 us
    reduce_scatter x2, waiting for transfers between devices, run_steps(): lax.psum_scatter(partial_value, 'dp', scatter_dimension=1, tiled=True)  49 us
    all_to_all x2, waiting for transfers between devices, run_steps(): lax.all_to_all(expert_out, 'expert', split_axis=1, concat_axis=1, tiled=T...  34.8 us
    all_to_all x2, starting transfers between devices, run_steps(): lax.all_to_all(packed, 'expert', split_axis=1, concat_axis=1, tiled=True)  18.7 us
  transfers between devices with their start and end apart: 10, of which 5 were waited for; matrix products, arithmetic and copies ran while one was open for 10% of the time, Pallas kernels for 0%

commit v1 on v0

v1 whole, which is shorter than its diff:
```python
import jax
import jax.numpy as jnp
from jax import lax
from jax.sharding import PartitionSpec as P

LANES = 128
CHUNK_BYTES = 16 << 20


def expert_weights(expert_ids, gate_probs, expert_count):
    hot = expert_ids[..., None] == lax.iota(jnp.int32, expert_count)
    return jnp.sum(jnp.where(hot, gate_probs[..., None], 0.0), axis=-2)


def relocate(pair_low, gate_up, down_proj):
    slot_count = lax.axis_size("expert")
    half = slot_count // 2

    def branch(low):
        perm = [(low, low + half), (low + half, low)]
        return lambda operands: tuple(lax.ppermute(o, "expert", perm) for o in operands)

    return lax.switch(pair_low, [branch(j) for j in range(half)], (gate_up, down_proj))


def expert_share(gathered, gate_up, down_proj, me, expert_count):
    units, width = down_proj.shape
    side_width = gathered.shape[1] - width
    column = lax.iota(jnp.int32, side_width)
    pick = (column == me) | (column == me + expert_count)
    weight = jnp.sum(jnp.where(pick, gathered[:, width:].astype(jnp.float32), 0.0), axis=-1)
    projected = lax.dot_general(
        gathered[:, :width],
        gate_up.reshape(2 * units, width),
        (((1,), (1,)), ((), ())),
        preferred_element_type=jnp.float32,
    )
    hidden = (jax.nn.silu(projected[:, :units]) * projected[:, units:]).astype(jnp.bfloat16)
    partial = jnp.dot(hidden, down_proj, preferred_element_type=jnp.float32)
    return (partial * weight[:, None]).astype(jnp.bfloat16)


def local(tokens, expert_ids, gate_probs, gate_up, down_proj, pairs):
    steps, rows, width = tokens.shape
    expert_count = lax.axis_size("expert")
    me = lax.axis_index("expert")
    pair_count = pairs.shape[0]
    axes = ("dp", "expert")

    weights = expert_weights(expert_ids, gate_probs, expert_count)
    high = weights.astype(jnp.bfloat16)
    low = (weights - high.astype(jnp.float32)).astype(jnp.bfloat16)
    side_width = -(-2 * expert_count // LANES) * LANES
    side = jnp.concatenate([high, low], axis=-1)
    side = jnp.pad(side, ((0, 0), (0, 0), (0, side_width - 2 * expert_count)))
    packed = jnp.concatenate([tokens, side], axis=-1).reshape(steps * rows, width + side_width)
    row_bytes = 2 * width * steps * rows * lax.axis_size("dp") * expert_count
    parts = 1
    while row_bytes > parts * CHUNK_BYTES and steps * rows % (32 * parts) == 0:
        parts *= 2
    pieces = packed.reshape(parts, steps * rows // parts, width + side_width)
    gathered = lax.all_gather(pieces[0], axes, axis=0, tiled=True)
    got = [relocate(pairs[0, 0], gate_up, down_proj)]
    gathered, got = lax.optimization_barrier((gathered, got))

    outs = []
    for part in range(parts):
        if part:
            piece, outs[-1] = lax.optimization_barrier((pieces[part], outs[-1]))
            gathered = lax.all_gather(piece, axes, axis=0, tiled=True)
        partial = expert_share(gathered, gate_up[0], down_proj[0], me, expert_count)
        outs.append(lax.psum_scatter(partial, axes, scatter_dimension=0, tiled=True))
    got += [relocate(pairs[p, 0], gate_up, down_proj) for p in range(1, min(2, pair_count))]
    out = jnp.stack(outs).reshape(steps, rows, width)

    def place(pair, arrived, placed):
        mine = jnp.any(pair == me)
        return tuple(jnp.where(mine, new, old) for new, old in zip(arrived, placed))

    placed = (gate_up, down_proj)
    for p, arrived in enumerate(got):
        placed = place(pairs[p], arrived, placed)
    if pair_count > len(got):
        placed = lax.fori_loop(
            len(got),
            pair_count,
            lambda p, held: place(pairs[p], relocate(pairs[p, 0], gate_up, down_proj), held),
            placed,
        )
    placed_gu, placed_down = placed
    return out, placed_gu, placed_down


def solution(mesh):
    return jax.shard_map(
        local,
        mesh=mesh,
        in_specs=(
            P(None, ("dp", "expert"), None),
            P(None, ("dp", "expert"), None),
            P(None, ("dp", "expert"), None),
            P("expert", None, "dp", None),
            P("expert", "dp", None),
            P(),
        ),
        out_specs=(
            P(None, ("dp", "expert"), None),
            P("expert", None, "dp", None),
            P("expert", "dp", None),
        ),
        check_vma=False,
    )
```

time: 678 us -> 341 us (0.50)
  waiting for transfers between devices: 538 us -> 274 us
  local copies, waits for them, and re-layouts: 44.3 us -> 2.82 us
  starting transfers between devices: 41.2 us -> 13.6 us
    all_to_all x4 -> x0, waiting for transfers between devices: 247 us -> none  [the longest x2 212 us: run_steps(): lax.all_to_all(packed, 'expert', split_axis=1, concat_axis=1, tiled=True)]
    ppermute x2 -> x4, waiting for transfers between devices: 242 us -> 142 us  [branch(): lax.ppermute(o, 'expert', perm)]
    reduce_scatter x2 -> x1, waiting for transfers between devices: 49 us -> 132 us  [local(): lax.psum_scatter(partial, axes, scatter_dimension=0, tiled=True)]
    all_to_all x4 -> x0, starting transfers between devices: 28.1 us -> none  [the longest x2 18.7 us: run_steps(): lax.all_to_all(packed, 'expert', split_axis=1, concat_axis=1, tiled=True)]
    another operation x8 -> x0, local copies, waits for them, and re-layouts: 24.2 us -> none  [the longest x2 9.38 us: run_steps(): received[0].reshape(-1, feature_dim)]
    all_gather x2 -> x0, local copies, waits for them, and re-layouts: 10.4 us -> none  [run_steps(): received = lax.all_gather(arrived[:, None], 'dp', axis=1, tiled=True)]
    dot_general x6 -> x2, matrix products: 18.8 us -> 17.9 us  [the longest x1 11.1 us: expert_share(): lax.dot_general(gathered[:, :width], gate_up.reshape(2 * units, width), (...]
  transfers between devices with their start and end apart: 10 -> 6, of which waited for: 5 -> 2; matrix products, arithmetic and copies ran while one was open for 10% -> 4% of each run, Pallas kernels for 0% -> 0%
where the time goes in v1:
time: 341 us; the launch traced here: 340 us
  waiting for transfers between devices  274 us (80%)
  matrix products  17.9 us (5%)
  other arithmetic  16.7 us (5%)
  between operations  15.4 us (5%)
  starting transfers between devices  13.6 us (4%)
    ppermute x4, waiting for transfers between devices, branch(): lax.ppermute(o, 'expert', perm)  142 us
    reduce_scatter x1, waiting for transfers between devices, local(): lax.psum_scatter(partial, axes, scatter_dimension=0, tiled=True)  132 us
    ppermute x4, starting transfers between devices, branch(): lax.ppermute(o, 'expert', perm)  13.5 us
    select_n x2, other arithmetic, place(): jnp.where(mine, new, old)  12.9 us
    dot_general x1, matrix products, expert_share(): lax.dot_general(gathered[:, :width], gate_up.reshape(2 * units, width), (...  11.1 us
  transfers between devices with their start and end apart: 6, of which 2 were waited for; matrix products, arithmetic and copies ran while one was open for 4% of the time, Pallas kernels for 0%

profile of v1, /device:TPU:0, one launch (start us, length us, event | category | flops | bytes accessed | tf_op | source)
XLA Modules:
  0.0 340.1 jit_solution(9753735800164317290)
XLA Ops:
  7.2 0.0 all-gather.2.cloned.1.call-start
  7.2 0.8 copy.12
  8.0 0.8 copy.11
  8.8 0.1 select_reduce_fusion.1
  8.9 0.1 fusion.8
  9.0 1.7 pad_maximum_fusion
  10.7 0.0 all-gather.2.cloned.1.call-update
  10.7 0.0 reduce-scatter.2.cloned.1.call-start
  10.8 1.3 fusion.10
  12.7 149.6 %conditional.2 = (bf16[1,2,384,4096]{3,2,1,0:T(8,128)(2,1)}, bf16[1,384,4096]{2,1,0:T(8,128)(2,1)}) conditional(s32[]{:T(128)} %bitcast.1, (bf16[1,2,384,4096]{3,2,1,0:T(8,128)(2,1)}, bf16[1,384,4096]{2,1,0:T(8,128)(2,1)}) %tuple.73, (bf16[1,2,384,4096]{3,2,1,0:T(8,128)(2,1)}, ...), branch_computations={%region_1.2_spmd, %region_2.3_spmd, %region_3.4_spmd, %region_4.5_... | conditional | bytes 37748832 | solution.py:23
  12.7 5.9 %collective-permute-start = (bf16[1,2,384,4096]{3,2,1,0:T(8,128)(2,1)}, bf16[1,2,384,4096]{3,2,1,0:T(8,128)(2,1)}, u32[]{:S(2)}, u32[]{:S(2)}) collective-permute-start(bf16[1,2,384,4096]{3,2,1,0:T(8,128)(2,1)} %get-tuple-element.64), channel_id=1, source_target_pairs={{0,8},{8,0},{16,24},{24,16}} | collective-permute-start | bytes 18874376 | tf_op jit(solution)/shard_map/cond/branch_0_fun/ppermute | solution.py:21
  18.6 1.9 collective-permute-start.1
  20.6 141.7 %collective-permute-done.1 = bf16[1,384,4096]{2,1,0:T(8,128)(2,1)} collective-permute-done((bf16[1,384,4096]{2,1,0:T(8,128)(2,1)}, bf16[1,384,4096]{2,1,0:T(8,128)(2,1)}, u32[]{:S(2)}, u32[]{:S(2)}) %collective-permute-start.1) | collective-permute-done | bytes 3145760 | tf_op jit(solution)/shard_map/cond/branch_0_fun/ppermute | solution.py:21
  162.2 0.0 collective-permute-done
  162.3 0.0 all-gather.2.cloned.1.call-done
  162.3 1.1 select_reduce_fusion
  163.4 0.0 copy-start
  163.4 11.1 %fusion = f32[1024,768]{1,0:T(8,128)S(1)} fusion(bf16[768,4096]{1,0:T(8,128)(2,1)} %bitcast.9, bf16[1024,4224]{1,0:T(8,128)(2,1)} %all-gather.2.cloned.1.call-done), kind=kOutput, calls=%fused_computation.1 | convolution fusion | flops 6442450944 | bytes 17825792 | tf_op jit(solution)/shard_map/dot_general | solution.py:32
  174.5 0.0 copy-done
  174.5 6.8 %multiply_convert_fusion = bf16[1024,4096]{1,0:T(8,128)(2,1)} fusion(f32[1024]{0:T(1024)S(1)} %select_reduce_fusion, bf16[1,384,4096]{2,1,0:T(8,128)(2,1)S(1)} %copy-done, f32[1024,768]{1,0:T(8,128)S(1)} %fusion), kind=kOutput, calls=%fused_computation | convolution fusion | flops 3231973376 | bytes 14684160 | tf_op jit(solution)/shard_map/dot_general | solution.py:39
  181.3 0.0 copy-start.1
  181.3 0.0 reduce-scatter.2.cloned.1.call-update
  182.0 5.7 %conditional.3 = (bf16[1,2,384,4096]{3,2,1,0:T(8,128)(2,1)}, bf16[1,384,4096]{2,1,0:T(8,128)(2,1)}) conditional(s32[]{:T(128)} %bitcast.5, (bf16[1,2,384,4096]{3,2,1,0:T(8,128)(2,1)}, bf16[1,384,4096]{2,1,0:T(8,128)(2,1)S(1)}) %tuple.99, (bf16[1,2,384,4096]{3,2,1,0:T(8,128)(2,1)}, ...), branch_computations={%region_12.13_spmd, %region_13.14_spmd, %region_14.15_spmd, %regio... | conditional | bytes 37748832 | solution.py:23
  182.0 3.3 collective-permute-start.30
  185.2 2.4 collective-permute-start.31
  187.7 0.0 collective-permute-done.31
  187.7 0.0 collective-permute-done.30
  187.7 0.0 copy-done.1
  187.7 0.7 compare_reduce_fusion.1
  188.4 5.3 %select_select_fusion.1 = bf16[1,384,4096]{2,1,0:T(8,128)(2,1)} fusion(bf16[1,384,4096]{2,1,0:T(8,128)(2,1)} %get-tuple-element.111, bf16[1,384,4096]{2,1,0:T(8,128)(2,1)} %get-tuple-element.112, bf16[1,384,4096]{2,1,0:T(8,128)(2,1)S(1)} %copy-done, pred[]{:T(512)} %get-tuple-element.114, pred[]{:T(512)} %get-tuple-element.113), kind=kLoop, calls=%fused_computation.5 | loop fusion | flops 3145728 | bytes 12582914 | tf_op jit(solution)/shard_map/jit(_where)/select_n | solution.py:78
  193.7 7.7 %select_select_fusion = bf16[1,2,384,4096]{3,2,1,0:T(8,128)(2,1)} fusion(bf16[1,2,384,4096]{3,2,1,0:T(8,128)(2,1)} %get-tuple-element.109, bf16[1,2,384,4096]{3,2,1,0:T(8,128)(2,1)} %get-tuple-element.110, bf16[1,2,384,4096]{3,2,1,0:T(8,128)(2,1)} %param.25, pred[]{:T(512)} %get-tuple-element.114, pred[]{:T(512)} %get-tuple-element.113), kind=kLoop, calls=%fused_computation.3 | loop fusion | flops 6291456 | bytes 25165826 | tf_op jit(solution)/shard_map/jit(_where)/select_n | solution.py:78
  201.3 131.9 %reduce-scatter.2.cloned.1.call-done = bf16[32,4096]{1,0:T(8,128)(2,1)} async-done(((bf16[1024,4096]{1,0:T(8,128)(2,1)}), bf16[32,4096]{1,0:T(8,128)(2,1)}) %reduce-scatter.2.cloned.1.call-update) | async-done | bytes 262160 | tf_op jit(solution)/shard_map/reduce_scatter | solution.py:72
  (2 shorter events, 0.0 us)
Async XLA Ops:
  7.2 155.1 %all-gather.2.cloned.1.call-start = ((), (), s32[]{:S(2)}) async-start(), calls=%async_computation.1 | async-start | bytes 8921088 | tf_op jit(solution)/shard_map/all_gather | solution.py:62
  10.7 322.5 %reduce-scatter.2.cloned.1.call-start = ((), (), s32[]{:S(2)}) async-start(), calls=%async_computation.2 | async-start | bytes 8650752 | tf_op jit(solution)/shard_map/reduce_scatter | solution.py:72
  12.7 149.6 %collective-permute-start = (bf16[1,2,384,4096]{3,2,1,0:T(8,128)(2,1)}, bf16[1,2,384,4096]{3,2,1,0:T(8,128)(2,1)}, u32[]{:S(2)}, u32[]{:S(2)}) collective-permute-start(bf16[1,2,384,4096]{3,2,1,0:T(8,128)(2,1)} %get-tuple-element.64), channel_id=1, source_target_pairs={{0,8},{8,0},{16,24},{24,16}} | collective-permute-start | bytes 18874376 | tf_op jit(solution)/shard_map/cond/branch_0_fun/ppermute | solution.py:21
  18.6 143.6 %collective-permute-start.1 = (bf16[1,384,4096]{2,1,0:T(8,128)(2,1)}, bf16[1,384,4096]{2,1,0:T(8,128)(2,1)}, u32[]{:S(2)}, u32[]{:S(2)}) collective-permute-start(bf16[1,384,4096]{2,1,0:T(8,128)(2,1)} %get-tuple-element.65), channel_id=1, source_target_pairs={{0,8},{8,0},{16,24},{24,16}} | collective-permute-start | bytes 9437192 | tf_op jit(solution)/shard_map/cond/branch_0_fun/ppermute | solution.py:21
  163.4 11.1 %copy-start = (bf16[1,384,4096]{2,1,0:T(8,128)(2,1)S(1)}, bf16[1,384,4096]{2,1,0:T(8,128)(2,1)}, u32[]{:S(2)}) copy-start(bf16[1,384,4096]{2,1,0:T(8,128)(2,1)} %param.26) | copy-start | bytes 9437188
  181.3 6.4 %copy-start.1 = (s32[2,2]{1,0:T(2,128)S(1)}, s32[2,2]{1,0:T(2,128)}, u32[]{:S(2)}) copy-start(s32[2,2]{1,0:T(2,128)} %param.27) | copy-start | bytes 52
  182.0 5.7 %collective-permute-start.30 = (bf16[1,2,384,4096]{3,2,1,0:T(8,128)(2,1)}, bf16[1,2,384,4096]{3,2,1,0:T(8,128)(2,1)}, u32[]{:S(2)}, u32[]{:S(2)}) collective-permute-start(bf16[1,2,384,4096]{3,2,1,0:T(8,128)(2,1)} %get-tuple-element.94), channel_id=1, source_target_pairs={{7,15},{15,7},{23,31},{31,23}} | collective-permute-start | bytes 18874376 | tf_op jit(solution)/shard_map/cond/branch_7_fun/ppermute | solution.py:21
  185.2 2.4 collective-permute-start.31
Sparse Core Ops, SparseCore 0:
  11.5 89.5 all-gather.1
  181.4 151.7 reduce-scatter.1
